TPU v7x, 32 devices: a whole 2x2x4 slice. The times are simulated.
32 devices in a mesh: seq: 4 (over y, x), tp: 8 (over z, core).
Axes of the slice: x: 2, y: 2, z: 4, core: 2. Of those that a mesh axis runs over, the one named last changes fastest.
Arguments:
- hidden_in: bfloat16 [1024, 5120], P('seq', 'tp'), may hold values from -16 to 16
- seg_ids: int32 [1024], P('seq'), may hold values from 0 to 3, never falling along the last dimension, each value on 1 to 640 neighbouring positions
- positions: int32 [3, 1024], P(None, 'seq'), may hold values from 0 to 63
- mod_table: float32 [4, 3, 5120], P(None, None, 'tp'), may hold values from -4 to 4
- w_qkv: bfloat16 [5120, 3, 4096], P('seq', None, 'tp')
- q_gain: float32 [4096], P('tp'), may hold values from 0.5 to 3.5
- k_gain: float32 [4096], P('tp'), may hold values from 0.5 to 3.5
- w_out: bfloat16 [4096, 5120], P('tp', 'seq'), may hold values from -0.125 to 0.125
Outputs:
- hidden_out: bfloat16 [1024, 5120], P('seq', 'tp')
- k_cache: bfloat16 [1024, 4096], P('seq', 'tp')
- v_cache: bfloat16 [1024, 4096], P('seq', 'tp')
Inputs may be any that keep to these rules, and one draw needn't show every extreme that they name: `seg_ids`: segment ids never fall along the stream; each segment holds 1 to 640 tokens, and one holds exactly 640.
All inputs are finite; a program needn't handle non-finite values.
Results may differ from a plain program's by a relative error of at most 0.018.
Values may be sent and summed in bfloat16 or wider, within the bound.
A program may use at most 64 MiB of HBM per device.

v0:
```python
import functools
import math

import jax
import jax.numpy as jnp
import numpy as np
from jax import lax
from jax.experimental import pallas as pl
from jax.experimental.pallas import tpu as pltpu
from jax.sharding import PartitionSpec as P

HEAD_DIM = 128


EPSILON = 1e-06
NEG_FILL = -1e30


def rope_tables(positions):
    part_width = HEAD_DIM // 6
    widths = (HEAD_DIM - 4 * part_width, 2 * part_width, 2 * part_width)
    angle_list = []
    for axis_number in range(3):
        exponent = jnp.arange(0, widths[axis_number], 2, dtype=jnp.float32) / widths[axis_number]
        frequency = 1.0 / 10000.0**exponent
        angle_list.append(positions[axis_number].astype(jnp.float32)[:, None] * frequency[None, :])
    angle_all = jnp.concatenate(angle_list, axis=1)
    return (jnp.cos(angle_all), jnp.sin(angle_all))


def rotate_pairs(field, cosine, sine):
    even_part = field[..., 0::2]
    odd_part = field[..., 1::2]
    cos_wide = cosine[:, None, :]
    sin_wide = sine[:, None, :]
    new_even = even_part * cos_wide - odd_part * sin_wide
    new_odd = even_part * sin_wide + odd_part * cos_wide
    return jnp.stack([new_even, new_odd], axis=-1).reshape(field.shape)


def empty_state(query_rows, heads_here):
    maxima = jnp.full((heads_here, query_rows), NEG_FILL, jnp.float32)
    totals = jnp.zeros((heads_here, query_rows), jnp.float32)
    weighted = jnp.zeros((heads_here, query_rows, HEAD_DIM), jnp.float32)
    return (maxima, totals, weighted)


def merge_states(first, second):
    largest = jnp.maximum(first[0], second[0])
    first_factor = jnp.exp(first[0] - largest)
    second_factor = jnp.exp(second[0] - largest)
    totals = first[1] * first_factor + second[1] * second_factor
    weighted = first[2] * first_factor[..., None] + second[2] * second_factor[..., None]
    return (largest, totals, weighted)


def block_state(q_heads, seg_q, key_heads, value_heads, seg_k):
    score_scale = 1.0 / math.sqrt(HEAD_DIM)
    scores = (
        jnp.einsum("qhd,khd->hqk", q_heads, key_heads, preferred_element_type=jnp.float32)
        * score_scale
    )
    same_seg = seg_q[:, None] == seg_k[None, :]
    masked = jnp.where(same_seg[None], scores, NEG_FILL)
    maxima = jnp.max(masked, axis=2)
    weights = jnp.where(same_seg[None], jnp.exp(masked - maxima[..., None]), 0.0)
    totals = jnp.sum(weights, axis=2)
    weighted = jnp.einsum(
        "hqk,khd->hqd",
        weights.astype(jnp.bfloat16),
        value_heads,
        preferred_element_type=jnp.float32,
    )
    return (maxima, totals, weighted)


def absorb_keys(carry_state, q_heads, seg_q, key_rows, value_rows, seg_k):
    row_count = key_rows.shape[0]
    heads_here = q_heads.shape[1]
    block_rows = 512
    block_count = row_count // block_rows
    key_blocks = key_rows.reshape(block_count, block_rows, heads_here, HEAD_DIM)
    value_blocks = value_rows.reshape(block_count, block_rows, heads_here, HEAD_DIM)
    seg_blocks = seg_k.reshape(block_count, block_rows)

    def step_block(state_now, operands):
        key_block, value_block, seg_block = operands
        return (
            merge_states(state_now, block_state(q_heads, seg_q, key_block, value_block, seg_block)),
            None,
        )

    return lax.scan(step_block, carry_state, (key_blocks, value_blocks, seg_blocks))[0]


def body(hidden_in, seg_ids, positions, mod_table, w_qkv, q_gain, k_gain, w_out):
    tok_rows, feat_local = hidden_in.shape
    model_width = feat_local * lax.axis_size("tp")
    heads_width = w_qkv.shape[2]
    heads_here = heads_width // HEAD_DIM
    all_heads_width = heads_width * lax.axis_size("tp")
    x_float = hidden_in.astype(jnp.float32)
    row_sums, row_squares = lax.psum(
        (jnp.sum(x_float, axis=1), jnp.sum(x_float * x_float, axis=1)), "tp"
    )
    mean_value = row_sums / model_width
    variance = row_squares / model_width - mean_value * mean_value
    normed = (x_float - mean_value[:, None]) * lax.rsqrt(variance[:, None] + EPSILON)
    segment_count = mod_table.shape[0]
    table = mod_table.reshape(segment_count, 3 * feat_local)
    onehot = (seg_ids[:, None] == jnp.arange(segment_count, dtype=jnp.int32)[None, :]).astype(
        jnp.float32
    )
    modulation = jnp.dot(onehot, table, precision=lax.Precision.HIGHEST).reshape(
        tok_rows, 3, feat_local
    )
    modded = (normed * (1.0 + modulation[:, 1]) + modulation[:, 0]).astype(jnp.bfloat16)
    full_rows = lax.all_gather(modded, "tp", axis=1, tiled=True)
    portion = lax.all_gather(w_qkv, "seq", axis=0, tiled=True)
    flat = portion.reshape(portion.shape[0], 3 * heads_width)
    projected = jnp.dot(full_rows, flat, preferred_element_type=jnp.float32)
    query_f = projected[:, :heads_width]
    key_f = projected[:, heads_width : 2 * heads_width]
    value_f = projected[:, 2 * heads_width :]
    query_sq, key_sq = lax.psum(
        (jnp.sum(query_f * query_f, axis=1), jnp.sum(key_f * key_f, axis=1)), "tp"
    )
    query_n = query_f * lax.rsqrt(query_sq / all_heads_width + EPSILON)[:, None] * q_gain[None, :]
    key_n = key_f * lax.rsqrt(key_sq / all_heads_width + EPSILON)[:, None] * k_gain[None, :]
    cosine, sine = rope_tables(positions)
    q_heads = rotate_pairs(query_n.reshape(tok_rows, heads_here, HEAD_DIM), cosine, sine).astype(
        jnp.bfloat16
    )
    k_heads = rotate_pairs(key_n.reshape(tok_rows, heads_here, HEAD_DIM), cosine, sine).astype(
        jnp.bfloat16
    )
    k_cache = k_heads.reshape(tok_rows, heads_width)
    v_cache = value_f.astype(jnp.bfloat16)
    key_rows = lax.all_gather(k_cache, "seq", axis=0, tiled=True)
    value_rows = lax.all_gather(v_cache, "seq", axis=0, tiled=True)
    seg_k = lax.all_gather(seg_ids, "seq", axis=0, tiled=True)
    state_end = absorb_keys(
        empty_state(tok_rows, heads_here), q_heads, seg_ids, key_rows, value_rows, seg_k
    )
    attention = (state_end[2] / state_end[1][..., None]).transpose(1, 0, 2)
    attn_out = attention.reshape(tok_rows, heads_width).astype(jnp.bfloat16)
    terms = jnp.dot(
        attn_out,
        lax.all_gather(w_out, "seq", axis=1, tiled=True),
        preferred_element_type=jnp.float32,
    )
    mixed = lax.psum_scatter(
        terms.astype(jnp.bfloat16), "tp", scatter_dimension=1, tiled=True
    ).astype(jnp.float32)
    hidden_out = (x_float + modulation[:, 2] * mixed).astype(jnp.bfloat16)
    return (hidden_out, k_cache, v_cache)


MESH = pl.DeviceIdType.MESH
EXACT = lax.Precision.HIGHEST
FAR = -1e30
CHUNKS = 4


def dot00(a, b):
    return lax.dot_general(
        a, b, (((0,), (0,)), ((), ())), precision=EXACT, preferred_element_type=jnp.float32
    )


def dot11(a, b, precision=None):
    return lax.dot_general(
        a, b, (((1,), (1,)), ((), ())), precision=precision, preferred_element_type=jnp.float32
    )


def fused(
    n_seq, n_tp, width, all_heads,
    hid, segs, positions, modt, freq, w_any, q_gain, k_gain, w_out_any,
    out, k_out, v_out,
    w, w_out, mod8, meta_all, st1, gathered, full, part, relay, parts_in, parts_last,
    st2, st3, qkv, cosine, sine, q_ext, k_ext, v_all, attn, terms, pair_in, summed, moved,
    arrived, joint, joined, part_v, relay_v, v_in, v_last, gate,
    w_sem, j_r, pv_s, pv_r, lv_s, lv_r, meta_s, meta_r, st1_s, st1_r, z_s, z_r, f_s, f_r, swap_s, swap_r, p_s, p_r,
    last_s, last_r, st2_s, st2_r, st3_s, st3_r, k_s, k_r, v_s, v_r, a_s, a_r, pair_s, pair_r,
    mv_s, mv_r, ar_s, ar_r,
):
    s = lax.axis_index("seq")
    t = lax.axis_index("tp")
    z = t // 2
    c = t % 2
    rows, feats = hid.shape
    n_z = n_tp // 2
    chunks = CHUNKS
    cr = rows // chunks
    many = n_seq * cr
    sibling = z * 2 + 1 - c
    x_next = (s // 2) * 2 + 1 - s % 2
    y_next = (1 - s // 2) * 2 + s % 2
    corner = (1 - s // 2) * 2 + 1 - s % 2

    def copy(src, dst, send, recv, to_s, to_t):
        return pltpu.make_async_remote_copy(
            src_ref=src, dst_ref=dst, send_sem=send, recv_sem=recv,
            device_id=(to_s, to_t), device_id_type=MESH,
        )

    def chunk(i):
        return pl.ds(pl.multiple_of(i * cr, cr), cr)

    def lanes_of(h):
        return pl.ds(pl.multiple_of(h * 128, 128), 128)

    plane = [(s + d) % n_seq for d in range(1, n_seq)]
    column = [(t + d) % n_tp for d in range(1, n_tp)]
    line = [(z + jnp.where(z < n_z // 2, d, n_z - d)) % n_z for d in range(1, n_z)]

    def apart(p):
        return (p + z == n_z - 1) & (p * z == 0)

    def between(p):
        return ((z == n_z - 2) & (p == 0)) | ((z == 1) & (p == n_z - 1))

    barrier = pltpu.get_barrier_semaphore()
    for p in plane:
        pl.semaphore_signal(barrier, inc=1, device_id=(p, t), device_id_type=MESH)
    for p in column:
        pl.semaphore_signal(barrier, inc=1, device_id=(s, p), device_id_type=MESH)
    load_w = pltpu.make_async_copy(w_any, w, w_sem.at[0])
    load_w_out = pltpu.make_async_copy(w_out_any, w_out, w_sem.at[1])
    load_w.start()
    load_w_out.start()

    x = hid[...].astype(jnp.float32)
    row8 = lax.broadcasted_iota(jnp.int32, (8, rows), 0)
    ones_b = jnp.ones((8, feats), jnp.bfloat16)
    ones_f = jnp.ones((8, feats), jnp.float32)
    st1[t] = jnp.where(row8 == 0, dot11(ones_b, hid[...]), dot11(ones_f, x * x, EXACT))
    meta_all[s] = jnp.zeros((8, rows), jnp.float32)
    meta_all[s, 0:3] = positions[...].astype(jnp.float32)
    meta_all[s, 3:4] = segs[...].astype(jnp.float32)
    pl.semaphore_wait(barrier, n_seq - 1 + n_tp - 1)
    for p in column:
        copy(st1.at[t], st1.at[t], st1_s.at[p], st1_r.at[t], s, p).start()
    for p in plane:
        copy(meta_all.at[s], meta_all.at[s], meta_s.at[p], meta_r.at[s], p, t).start()

    onehot = (segs[...] == row8).astype(jnp.float32)
    mod8[...] = jnp.zeros(mod8.shape, jnp.float32)
    mod8[:, : modt.shape[1]] = modt[...]
    shift = dot00(onehot, mod8[0])
    scale = dot00(onehot, mod8[1])
    gate[...] = dot00(onehot, mod8[2])

    for p in column:
        copy(st1.at[p], st1.at[p], st1_s.at[p], st1_r.at[p], s, p).wait_recv()
    totals = jnp.sum(st1[...], axis=0)
    mean_row = totals[0:1] / width
    scale_row = lax.rsqrt(totals[1:2] / width - mean_row * mean_row + EPSILON)
    both = jnp.where(row8 == 0, mean_row, jnp.where(row8 == 1, scale_row, 0.0))
    pick = lax.broadcasted_iota(jnp.int32, (8, 128), 0)
    mean_col = dot00(both, (pick == 0).astype(jnp.float32))[:, 0:1]
    scale_col = dot00(both, (pick == 1).astype(jnp.float32))[:, 0:1]
    normed = (x - mean_col) * scale_col
    gathered[z] = (normed * (1.0 + scale) + shift).astype(jnp.bfloat16)

    def own_block(i, p):
        mine = gathered.at[z, chunk(i)]
        return copy(mine, mine, z_s.at[i, p], z_r.at[i, z], s, p * 2 + c)

    def block_on(i, p):
        theirs = gathered.at[p, chunk(i)]
        return copy(theirs, theirs, z_s.at[i, z], z_r.at[i, p], s, (n_z - 1 - p) * 2 + c)

    for i in range(chunks):
        for p in line:
            @pl.when(jnp.logical_not(apart(p)))
            def _():
                own_block(i, p).start()

    for p in plane:
        copy(meta_all.at[p], meta_all.at[p], meta_s.at[p], meta_r.at[p], p, t).wait_recv()
    lane = lax.broadcasted_iota(jnp.int32, (rows, 128), 1)
    even = lane % 2 == 0

    def pass_on(i, p):
        @pl.when(p == s)
        def _():
            full[c, s, chunk(i)] = gathered[p, chunk(i)]

        @pl.when(p != s)
        def _():
            copy(
                gathered.at[p, chunk(i)], full.at[c, s, chunk(i)], f_s.at[i, p], f_r.at[i, s], p, t
            ).start()

    def from_line(i):
        pass_on(i, z)
        for p in line:
            theirs = gathered.at[p, chunk(i)]
            copy(theirs, theirs, z_s.at[i, p], z_r.at[i, p], s, p * 2 + c).wait_recv()

            @pl.when(between(p))
            def _():
                block_on(i, p).start()

            pass_on(i, p)

    def swap(i, half):
        block = full.at[half, :, chunk(i)]
        return copy(block, block, swap_s.at[i], swap_r.at[i], s, sibling)

    def from_plane(i):
        for p in plane:
            theirs = full.at[c, p, chunk(i)]
            copy(theirs, theirs, f_s.at[i, p], f_r.at[i, p], p, t).wait_recv()
        swap(i, c).start()

    def tables(j):
        block = meta_all[j]
        angle = dot00(block, freq[...])
        cosine[:, j] = jnp.cos(angle).reshape(chunks, cr, 128)
        sine[:, j] = (jnp.where(even, -1.0, 1.0) * jnp.sin(angle)).reshape(chunks, cr, 128)
        seg = dot00(block, (pick == 3).astype(jnp.float32))
        same = seg == lane.astype(jnp.float32)
        q_mask = same.astype(jnp.float32).astype(jnp.bfloat16)
        k_mask = jnp.where(same | (lane >= 8), 0.0, FAR).astype(jnp.bfloat16)
        q_ext[:, j, :, 128:] = q_mask.reshape(chunks, cr, 128)
        k_ext[:, j, :, 128:] = k_mask.reshape(chunks, cr, 128)

    def first_of(i):
        return jnp.where(i % 2 == 0, x_next, y_next)

    def second_of(i):
        return jnp.where(i % 2 == 0, y_next, x_next)

    qk_bufs = (part, parts_in, relay, parts_last, p_s, p_r, last_s, last_r)
    v_bufs = (part_v, v_in, relay_v, v_last, pv_s, pv_r, lv_s, lv_r)

    def to_first(bufs, i, n, h):
        own, got, _, _, send, recv, _, _ = bufs
        return copy(own.at[i, h], got.at[i, n], send.at[i, n], recv.at[i, n], first_of(i), t)

    def to_second(bufs, i):
        _, _, passed, got, _, _, send, recv = bufs
        return copy(passed.at[i], got.at[i], send.at[i], recv.at[i], second_of(i), t)

    def project(bufs, fields, i):
        left = full[0, :, chunk(i)].reshape(many, feats)
        right = full[1, :, chunk(i)].reshape(many, feats)
        for at, n in enumerate(fields):
            acc = jnp.dot(left, w[n, :feats], preferred_element_type=jnp.float32)
            acc += jnp.dot(right, w[n, feats:], preferred_element_type=jnp.float32)
            for h in range(n_seq):
                bufs[0][i, h, :, at * 128 : (at + 1) * 128] = acc[
                    :, h * 128 : (h + 1) * 128
                ].astype(jnp.bfloat16)
        to_first(bufs, i, 1, corner).start()
        to_first(bufs, i, 0, first_of(i)).start()

    def project_qk(i):
        swap(i, 1 - c).wait_recv()
        project(qk_bufs, (0, 1), i)

    def project_v(i):
        project(v_bufs, (2,), i)

    def relay_on(bufs, i):
        own, got, passed = bufs[:3]
        to_first(bufs, i, 1, corner).wait_recv()
        passed[i] = (
            own[i, second_of(i)].astype(jnp.float32) + got[i, 1].astype(jnp.float32)
        ).astype(jnp.bfloat16)
        to_second(bufs, i).start()

    def summed_head(bufs, i):
        own, got, _, last = bufs[:4]
        to_first(bufs, i, 0, corner).wait_recv()
        to_second(bufs, i).wait_recv()
        total = own[i, s].astype(jnp.float32) + got[i, 0].astype(jnp.float32)
        return total + last[i].astype(jnp.float32)

    ones_h = jnp.ones((8, 128), jnp.float32)
    st2[s] = jnp.zeros((8, rows), jnp.float32)

    def collect(i):
        total = summed_head(qk_bufs, i)
        qkv[i] = total
        q_sq = dot11(ones_h, total[:, :128] * total[:, :128], EXACT)
        k_sq = dot11(ones_h, total[:, 128:256] * total[:, 128:256], EXACT)
        st2[s] = jnp.where(row8 == 2 * i, q_sq, jnp.where(row8 == 2 * i + 1, k_sq, st2[s]))

    def collect_v(i, carry):
        v_all[i] = summed_head(v_bufs, i).astype(jnp.bfloat16).reshape(n_seq, cr, 128)
        return carry

    load_w.wait()
    load_w_out.wait()

    def during(step, at, work):
        @pl.when((step >= at) & (step < at + chunks))
        def _():
            work(step - at)

    def project_step(step, carry):
        during(step, 0, from_line)
        during(step, 1, project_qk)
        during(step, 2, functools.partial(relay_on, qk_bufs))
        during(step, 0, from_plane)
        during(step, 0, tables)
        during(step, 3, project_v)
        during(step, 3, collect)
        return carry

    lax.fori_loop(0, chunks + 3, project_step, 0)

    for p in plane:
        copy(st2.at[s], st2.at[s], st2_s.at[p], st2_r.at[s], p, t).start()

    def relay_v_on(i, carry):
        relay_on(v_bufs, i)
        return carry

    lax.fori_loop(0, chunks, relay_v_on, 0)

    gains = (q_gain[pl.ds(s, 1), :], k_gain[pl.ds(s, 1), :])

    def rotate(i, carry):
        cos_i = cosine[i].reshape(many, 128)
        sin_i = sine[i].reshape(many, 128)
        for n in range(2):
            cols = slice(n * 128, (n + 1) * 128)
            field = qkv[i, :, cols] * gains[n]
            swapped = jnp.where(even, pltpu.roll(field, 127, 1), pltpu.roll(field, 1, 1))
            qkv[i, :, cols] = field * cos_i + swapped * sin_i
        return carry

    for p in plane:
        copy(st2.at[p], st2.at[p], st2_s.at[p], st2_r.at[p], p, t).wait_recv()
    st3[t] = jnp.sum(st2[...], axis=0)
    for p in column:
        copy(st3.at[t], st3.at[t], st3_s.at[p], st3_r.at[t], s, p).start()

    def send_v(p):
        return copy(v_all.at[:, p], v_out.at[:, :, lanes_of(s)], v_s.at[p], v_r.at[s], p, t)

    def send_k(p):
        mine = k_ext.at[:, p, :, pl.ds(0, 128)]
        return copy(mine, k_out.at[:, :, lanes_of(s)], k_s.at[p], k_r.at[s], p, t)

    lax.fori_loop(0, chunks, rotate, 0)
    lax.fori_loop(0, chunks, collect_v, 0)
    for p in column:
        copy(st3.at[p], st3.at[p], st3_s.at[p], st3_r.at[p], s, p).wait_recv()
    norm_rows = lax.rsqrt(jnp.sum(st3[...], axis=0) / all_heads + EPSILON)

    def scale_rows(i, carry):
        q_col = dot00(norm_rows, (pick == 2 * i).astype(jnp.float32))
        k_col = dot00(norm_rows, (pick == 2 * i + 1).astype(jnp.float32))
        q_i = (qkv[i, :, :128] * q_col).astype(jnp.bfloat16)
        k_i = (qkv[i, :, 128:256] * k_col).astype(jnp.bfloat16)
        q_ext[i, :, :, :128] = q_i.reshape(n_seq, cr, 128)
        k_ext[i, :, :, :128] = k_i.reshape(n_seq, cr, 128)
        return carry

    lax.fori_loop(0, chunks, scale_rows, 0)

    score_scale = 1.0 / math.sqrt(HEAD_DIM)

    def attend(i):
        keys = k_ext[...].reshape(n_seq * rows, 256)
        values = v_all[...].reshape(n_seq * rows, 128)
        scores = dot11(q_ext[i].reshape(many, 256), keys)
        top = jnp.max(scores, axis=1, keepdims=True)
        weights = jnp.exp((scores - top) * score_scale)
        denominator = jnp.sum(weights, axis=1, keepdims=True)
        mixed = jnp.dot(weights.astype(jnp.bfloat16), values, preferred_element_type=jnp.float32)
        done = (mixed / denominator).astype(jnp.bfloat16)
        attn[i, :, :, lanes_of(s)] = done.reshape(n_seq, cr, 128)
        for p in plane:
            mine = attn.at[i, :, :, lanes_of(s)]
            copy(mine, mine, a_s.at[i, p], a_r.at[i, s], p, t).start()

    def pair(i):
        return copy(
            terms.at[i, 1 - c], pair_in.at[i], pair_s.at[i], pair_r.at[i], s, sibling
        )

    def out_project(i):
        for p in plane:
            theirs = attn.at[i, :, :, lanes_of(p)]
            copy(theirs, theirs, a_s.at[i, p], a_r.at[i, p], p, t).wait_recv()
        for n in range(2):
            cols = slice(n * feats, (n + 1) * feats)
            product = jnp.dot(
                attn[i].reshape(many, n_seq * 128), w_out[:, cols],
                preferred_element_type=jnp.float32,
            )
            terms[i, n] = product.astype(jnp.bfloat16).reshape(n_seq, cr, feats)
        pair(i).start()

    def pair_sum(i):
        pair(i).wait_recv()
        summed[i] = (terms[i, c].astype(jnp.float32) + pair_in[i].astype(jnp.float32)).astype(
            jnp.bfloat16
        )
        moved[s, i] = summed[i, s]
        for p in plane:
            copy(summed.at[i, p], moved.at[s, i], mv_s.at[i, p], mv_r.at[i, s], p, t).start()

    def to_line(i, p):
        return copy(
            moved.at[p, i], arrived.at[z, i], ar_s.at[i, p], ar_r.at[i, z], s, p * 2 + c
        )

    def to_joint(i, p):
        via = jnp.where(z == 0, 1, n_z - 2)
        return copy(moved.at[p, i], joint.at[i], ar_s.at[i, p], j_r.at[i], s, via * 2 + c)

    def deliver(i, p):
        @pl.when(p == z)
        def _():
            arrived[z, i] = moved[p, i]

        @pl.when(apart(p))
        def _():
            to_joint(i, p).start()
            arrived[p, i] = jnp.zeros((cr, feats), jnp.bfloat16)

        @pl.when((p != z) & jnp.logical_not(apart(p)) & jnp.logical_not(between(p)))
        def _():
            to_line(i, p).start()

    def join(i):
        @pl.when((z > 0) & (z < n_z - 1))
        def _():
            p = jnp.where(z == 1, n_z - 1, 0)
            to_joint(i, p).wait_recv()
            joined[i] = (
                moved[p, i].astype(jnp.float32) + joint[i].astype(jnp.float32)
            ).astype(jnp.bfloat16)
            copy(
                joined.at[i], arrived.at[z, i], ar_s.at[i, p], ar_r.at[i, z], s, p * 2 + c
            ).start()

    def deliver_all(i):
        deliver(i, s)
        for p in plane:
            theirs = moved.at[p, i]
            copy(theirs, theirs, mv_s.at[i, p], mv_r.at[i, p], p, t).wait_recv()
            deliver(i, p)

    def attend_step(step, carry):
        during(step, 0, attend)
        during(step, 1, out_project)
        during(step, 3, join)
        during(step, 2, deliver_all)
        during(step, 1, pair_sum)
        return carry

    lax.fori_loop(0, chunks + 3, attend_step, 0)
    for p in plane:
        send_k(p).start()
        send_v(p).start()
    k_out[:, :, lanes_of(s)] = k_ext[:, s, :, :128]
    v_out[:, :, lanes_of(s)] = v_all[:, s]

    def finish(i, carry):
        for p in line:
            theirs = arrived.at[p, i]

            @pl.when(jnp.logical_not(apart(p)))
            def _():
                copy(theirs, theirs, ar_s.at[i, p], ar_r.at[i, p], s, p * 2 + c).wait_recv()

        mixed = arrived[0, i].astype(jnp.float32)
        for p in range(1, n_z):
            mixed += arrived[p, i].astype(jnp.float32)
        base = hid[chunk(i), :].astype(jnp.float32)
        out[chunk(i), :] = (base + gate[chunk(i), :] * mixed).astype(jnp.bfloat16)
        return carry

    lax.fori_loop(0, chunks, finish, 0)

    for p in plane:
        copy(
            k_ext.at[:, p, :, pl.ds(0, 128)], k_out.at[:, :, lanes_of(p)], k_s.at[p], k_r.at[p], p, t
        ).wait()
        copy(v_all.at[:, p], v_out.at[:, :, lanes_of(p)], v_s.at[p], v_r.at[p], p, t).wait()
        copy(meta_all.at[s], meta_all.at[s], meta_s.at[p], meta_r.at[s], p, t).wait_send()
        copy(st2.at[s], st2.at[s], st2_s.at[p], st2_r.at[s], p, t).wait_send()
    for p in column:
        copy(st1.at[t], st1.at[t], st1_s.at[p], st1_r.at[t], s, p).wait_send()
        copy(st3.at[t], st3.at[t], st3_s.at[p], st3_r.at[t], s, p).wait_send()

    def drain(i, carry):
        swap(i, c).wait_send()
        pair(i).wait_send()
        for bufs in (qk_bufs, v_bufs):
            to_first(bufs, i, 0, first_of(i)).wait_send()
            to_first(bufs, i, 1, corner).wait_send()
            to_second(bufs, i).wait_send()
        for p in line:
            @pl.when(jnp.logical_not(apart(p)))
            def _():
                own_block(i, p).wait_send()

            @pl.when(between(p))
            def _():
                block_on(i, p).wait_send()

            to_line(i, p).wait_send()
        for p in plane:
            copy(
                gathered.at[p, chunk(i)], full.at[c, s, chunk(i)], f_s.at[i, p], f_r.at[i, s], p, t
            ).wait_send()
            mine = attn.at[i, :, :, lanes_of(s)]
            copy(mine, mine, a_s.at[i, p], a_r.at[i, s], p, t).wait_send()
            copy(summed.at[i, p], moved.at[s, i], mv_s.at[i, p], mv_r.at[i, s], p, t).wait_send()
        return carry

    lax.fori_loop(0, chunks, drain, 0)


def hand_over(*refs):
    for i in range(3):
        refs[3 + i][...] = refs[i][...]


def frequencies():
    part_width = HEAD_DIM // 6
    widths = (HEAD_DIM - 4 * part_width, 2 * part_width, 2 * part_width)
    table = np.zeros((8, HEAD_DIM), np.float32)
    at = 0
    for axis_number, wide in enumerate(widths):
        exponent = np.arange(0, wide, 2, dtype=np.float32) / np.float32(wide)
        frequency = (1.0 / np.float32(10000.0) ** exponent).astype(np.float32)
        table[axis_number, at : at + wide] = np.repeat(frequency, 2)
        at += wide
    return table


def fused_body(hidden_in, seg_ids, positions, mod_table, w_qkv, q_gain, k_gain, w_out):
    n_seq = lax.axis_size("seq")
    n_tp = lax.axis_size("tp")
    rows, feats = hidden_in.shape
    depth, _, heads_width = w_qkv.shape
    bf16, f32 = jnp.bfloat16, jnp.float32
    n_z = n_tp // 2
    chunks = CHUNKS
    cr = rows // chunks
    many = n_seq * cr
    dma = pltpu.SemaphoreType.DMA
    scratch = [
        pltpu.VMEM((3, depth, heads_width), bf16),
        pltpu.VMEM(w_out.shape, bf16),
        pltpu.VMEM((3, 8, feats), f32),
        pltpu.VMEM((n_seq, 8, rows), f32),
        pltpu.VMEM((n_tp, 8, rows), f32),
        pltpu.VMEM((n_z, rows, feats), bf16),
        pltpu.VMEM((2, n_seq, rows, feats), bf16),
        pltpu.VMEM((chunks, n_seq, many, 256), bf16),
        pltpu.VMEM((chunks, many, 256), bf16),
        pltpu.VMEM((chunks, 2, many, 256), bf16),
        pltpu.VMEM((chunks, many, 256), bf16),
        pltpu.VMEM((n_seq, 8, rows), f32),
        pltpu.VMEM((n_tp, 8, rows), f32),
        pltpu.VMEM((chunks, many, 256), f32),
        pltpu.VMEM((chunks, n_seq, cr, 128), f32),
        pltpu.VMEM((chunks, n_seq, cr, 128), f32),
        pltpu.VMEM((chunks, n_seq, cr, 256), bf16),
        pltpu.VMEM((chunks, n_seq, cr, 256), bf16),
        pltpu.VMEM((chunks, n_seq, cr, 128), bf16),
        pltpu.VMEM((chunks, n_seq, cr, heads_width), bf16),
        pltpu.VMEM((chunks, 2, n_seq, cr, feats), bf16),
        pltpu.VMEM((chunks, n_seq, cr, feats), bf16),
        pltpu.VMEM((chunks, n_seq, cr, feats), bf16),
        pltpu.VMEM((n_seq, chunks, cr, feats), bf16),
        pltpu.VMEM((n_z, chunks, cr, feats), bf16),
        pltpu.VMEM((chunks, cr, feats), bf16),
        pltpu.VMEM((chunks, cr, feats), bf16),
        pltpu.VMEM((chunks, n_seq, many, 128), bf16),
        pltpu.VMEM((chunks, many, 128), bf16),
        pltpu.VMEM((chunks, 2, many, 128), bf16),
        pltpu.VMEM((chunks, many, 128), bf16),
        pltpu.VMEM((rows, feats), f32),
        dma((2,)),
        dma((chunks,)),
        dma((chunks, 2)),
        dma((chunks, 2)),
        dma((chunks,)),
        dma((chunks,)),
    ]
    wide = (chunks, n_seq)
    shapes = [
        (n_seq,), (n_tp,), (chunks, n_z), wide, (chunks,), (chunks, 2), (chunks,),
        (n_seq,), (n_tp,), (n_seq,), (n_seq,), wide, (chunks,), wide, (chunks, n_z),
    ]
    for shape in shapes:
        scratch += [dma(shape), dma(shape)]
    vmem = pl.BlockSpec(memory_space=pltpu.VMEM)
    whole = pl.BlockSpec(memory_space=pl.ANY)
    results = pl.pallas_call(
        functools.partial(fused, n_seq, n_tp, feats * n_tp, heads_width * n_tp),
        out_shape=(
            jax.ShapeDtypeStruct((rows, feats), bf16),
            jax.ShapeDtypeStruct((chunks, cr, heads_width), bf16),
            jax.ShapeDtypeStruct((chunks, cr, heads_width), bf16),
        ),
        in_specs=[vmem, vmem, vmem, vmem, vmem, whole, vmem, vmem, whole],
        out_specs=(vmem, vmem, vmem),
        scratch_shapes=scratch,
        compiler_params=pltpu.CompilerParams(
            collective_id=0, has_side_effects=True, vmem_limit_bytes=58 * 1024 * 1024
        ),
        cost_estimate=pl.CostEstimate(
            flops=6_000_000_000, bytes_accessed=8_000_000, transcendentals=1_200_000
        ),
    )(
        hidden_in, seg_ids.reshape(1, rows), positions, mod_table.transpose(1, 0, 2),
        jnp.asarray(frequencies()), w_qkv.transpose(1, 0, 2),
        q_gain.reshape(n_seq, HEAD_DIM), k_gain.reshape(n_seq, HEAD_DIM), w_out,
    )
    hidden, k_cache, v_cache = pl.pallas_call(
        hand_over,
        out_shape=tuple(jax.ShapeDtypeStruct(r.shape, r.dtype) for r in results),
        in_specs=[vmem] * 3,
        out_specs=(vmem,) * 3,
        cost_estimate=pl.CostEstimate(flops=0, bytes_accessed=1_700_000, transcendentals=0),
    )(*results)
    return (
        hidden,
        k_cache.reshape(rows, heads_width),
        v_cache.reshape(rows, heads_width),
    )


def pick_body(*operands):
    hidden_in, seg_ids, positions, mod_table, w_qkv = operands[:5]
    n_seq, n_tp = lax.axis_size("seq"), lax.axis_size("tp")
    fits = (
        n_tp == 2 * n_seq
        and n_seq == 4
        and w_qkv.shape[2] == n_seq * HEAD_DIM
        and w_qkv.shape[0] == 2 * hidden_in.shape[1]
        and hidden_in.shape[0] == 256
        and mod_table.shape[0] <= 8
    )
    return (fused_body if fits else body)(*operands)


def solution(mesh):
    in_specs = (
        P("seq", "tp"),
        P("seq"),
        P(None, "seq"),
        P(None, None, "tp"),
        P("seq", None, "tp"),
        P("tp"),
        P("tp"),
        P("tp", "seq"),
    )
    out_specs = (P("seq", "tp"), P("seq", "tp"), P("seq", "tp"))
    return jax.shard_map(pick_body, mesh=mesh, in_specs=in_specs, out_specs=out_specs, check_vma=False)
```

profile of v0, /device:TPU:14, one launch (start us, length us, event | category | flops | bytes accessed | tf_op | source)
XLA Modules:
  0.0 130.7 jit_solution(7293849945405040816)
XLA Ops:
  0.6 128.0 %shard_map.112 = (bf16[256,640]{1,0:T(8,128)(2,1)}, bf16[4,64,512]{2,1,0:T(8,128)(2,1)}, bf16[4,64,512]{2,1,0:T(8,128)(2,1)}) custom-call(bf16[256,640]{1,0:T(8,128)(2,1)} %hid.1, s32[1,256]{1,0:T(1,128)} %bitcast.13, s32[3,256]{1,0:T(4,128)} %positions.1, f32[3,4,640]{2,1,0:T(4,128)} %bitcast.10, f32[8,128]{1,0:T(8,128)} %constant.2.clone.freq, ...), custom_call_target="tpu_custom_call" | custom-call | flops 6000000000 | bytes 8000000 | tf_op jit(solution)/shard_map/pallas_call | solution.py:703
  128.6 2.0 %shard_map.113 = (bf16[256,640]{1,0:T(8,128)(2,1)}, bf16[4,64,512]{2,1,0:T(8,128)(2,1)}, bf16[4,64,512]{2,1,0:T(8,128)(2,1)}) custom-call(bf16[256,640]{1,0:T(8,128)(2,1)} %get-tuple-element.9.refs_0_, bf16[4,64,512]{2,1,0:T(8,128)(2,1)} %get-tuple-element.10.refs_1_, bf16[4,64,512]{2,1,0:T(8,128)(2,1)} %get-tuple-element.11.refs_2_), custom_call_target="tpu_custom_call" | custom-call | bytes 1700000 | tf_op jit(solution)/shard_map/pallas_call | solution.py:724
where the time goes:
time: 131 us
  Pallas kernels  130 us (99%)
    pallas_call x1, Pallas kernels, fused_body(): pl.pallas_call(functools.partial(fused, n_seq, n_tp, feats * n_tp, heads_...  128 us

commit v1 on v0

--- a/solution.py
+++ b/solution.py
@@ -160,6 +160,7 @@
 EXACT = lax.Precision.HIGHEST
 FAR = -1e30
 CHUNKS = 4
+PLACES = 64
 
 
 def dot00(a, b):
@@ -180,7 +181,7 @@
     out, k_out, v_out,
     w, w_out, mod8, meta_all, st1, gathered, full, part, relay, parts_in, parts_last,
     st2, st3, qkv, cosine, sine, q_ext, k_ext, v_all, attn, terms, pair_in, summed, moved,
-    arrived, joint, joined, part_v, relay_v, v_in, v_last, gate,
+    arrived, joint, joined, part_v, relay_v, v_in, v_last, lookup, gate,
     w_sem, j_r, pv_s, pv_r, lv_s, lv_r, meta_s, meta_r, st1_s, st1_r, z_s, z_r, f_s, f_r, swap_s, swap_r, p_s, p_r,
     last_s, last_r, st2_s, st2_r, st3_s, st3_r, k_s, k_r, v_s, v_r, a_s, a_r, pair_s, pair_r,
     mv_s, mv_r, ar_s, ar_r,
@@ -316,11 +317,23 @@
             copy(theirs, theirs, f_s.at[i, p], f_r.at[i, p], p, t).wait_recv()
         swap(i, c).start()
 
+    place_col = lax.broadcasted_iota(jnp.int32, (PLACES, 128), 0).astype(jnp.float32)
+    angle = place_col * (freq[0:1, :] + freq[1:2, :] + freq[2:3, :])
+    even_col = lax.broadcasted_iota(jnp.int32, (PLACES, 128), 1) % 2 == 0
+    cos_all = jnp.cos(angle)
+    sin_all = jnp.where(even_col, -1.0, 1.0) * jnp.sin(angle)
+    for a in range(3):
+        on_axis = freq[a : a + 1, :] > 0.0
+        lookup[a * PLACES : (a + 1) * PLACES, :128] = jnp.where(on_axis, cos_all, 0.0)
+        lookup[a * PLACES : (a + 1) * PLACES, 128:] = jnp.where(on_axis, sin_all, 0.0)
+
     def tables(j):
         block = meta_all[j]
-        angle = dot00(block, freq[...])
-        cosine[:, j] = jnp.cos(angle).reshape(chunks, cr, 128)
-        sine[:, j] = (jnp.where(even, -1.0, 1.0) * jnp.sin(angle)).reshape(chunks, cr, 128)
+        place = lax.broadcasted_iota(jnp.int32, (PLACES, rows), 0).astype(jnp.float32)
+        where = [(block[a : a + 1] == place).astype(jnp.float32) for a in range(3)]
+        found = dot00(jnp.concatenate(where, axis=0), lookup[...])
+        cosine[:, j] = found[:, :128].reshape(chunks, cr, 128)
+        sine[:, j] = found[:, 128:].reshape(chunks, cr, 128)
         seg = dot00(block, (pick == 3).astype(jnp.float32))
         same = seg == lane.astype(jnp.float32)
         q_mask = same.astype(jnp.float32).astype(jnp.bfloat16)
@@ -403,16 +416,16 @@
             work(step - at)
 
     def project_step(step, carry):
+        during(step, 2, project_qk)
+        during(step, 3, functools.partial(relay_on, qk_bufs))
+        during(step, 1, from_plane)
+        during(step, 4, project_v)
+        during(step, 4, collect)
+        during(step, 0, tables)
         during(step, 0, from_line)
-        during(step, 1, project_qk)
-        during(step, 2, functools.partial(relay_on, qk_bufs))
-        during(step, 0, from_plane)
-        during(step, 0, tables)
-        during(step, 3, project_v)
-        during(step, 3, collect)
         return carry
 
-    lax.fori_loop(0, chunks + 3, project_step, 0)
+    lax.fori_loop(0, chunks + 4, project_step, 0)
 
     for p in plane:
         copy(st2.at[s], st2.at[s], st2_s.at[p], st2_r.at[s], p, t).start()
@@ -551,14 +564,14 @@
             deliver(i, p)
 
     def attend_step(step, carry):
+        during(step, 4, join)
+        during(step, 3, deliver_all)
+        during(step, 2, pair_sum)
         during(step, 0, attend)
         during(step, 1, out_project)
-        during(step, 3, join)
-        during(step, 2, deliver_all)
-        during(step, 1, pair_sum)
         return carry
 
-    lax.fori_loop(0, chunks + 3, attend_step, 0)
+    lax.fori_loop(0, chunks + 4, attend_step, 0)
     for p in plane:
         send_k(p).start()
         send_v(p).start()
@@ -683,6 +696,7 @@
         pltpu.VMEM((chunks, many, 128), bf16),
         pltpu.VMEM((chunks, 2, many, 128), bf16),
         pltpu.VMEM((chunks, many, 128), bf16),
+        pltpu.VMEM((3 * PLACES, 256), f32),
         pltpu.VMEM((rows, feats), f32),
         dma((2,)),
         dma((chunks,)),

time: 131 us -> 128 us (0.977)
  Pallas kernels: 130 us -> 128 us
    pallas_call x1, Pallas kernels: 128 us -> 126 us  [fused_body(): pl.pallas_call(functools.partial(fused, n_seq, n_tp, feats * n_tp, heads_...]
where the time goes in v1:
time: 128 us
  Pallas kernels  128 us (100%)
    pallas_call x1, Pallas kernels, fused_body(): pl.pallas_call(functools.partial(fused, n_seq, n_tp, feats * n_tp, heads_...  126 us

profile of v1, /device:TPU:14, one launch (start us, length us, event | category | flops | bytes accessed | tf_op | source)
XLA Modules:
  0.0 128.3 jit_solution(1621399449153764864)
XLA Ops:
  0.6 125.6 %shard_map.112 = (bf16[256,640]{1,0:T(8,128)(2,1)}, bf16[4,64,512]{2,1,0:T(8,128)(2,1)}, bf16[4,64,512]{2,1,0:T(8,128)(2,1)}) custom-call(bf16[256,640]{1,0:T(8,128)(2,1)} %hid.1, s32[1,256]{1,0:T(1,128)} %bitcast.13, s32[3,256]{1,0:T(4,128)} %positions.1, f32[3,4,640]{2,1,0:T(4,128)} %bitcast.10, f32[8,128]{1,0:T(8,128)} %constant.2.clone.freq, ...), custom_call_target="tpu_custom_call" | custom-call | flops 6000000000 | bytes 8000000 | tf_op jit(solution)/shard_map/pallas_call | solution.py:717
  126.2 2.0 %shard_map.113 = (bf16[256,640]{1,0:T(8,128)(2,1)}, bf16[4,64,512]{2,1,0:T(8,128)(2,1)}, bf16[4,64,512]{2,1,0:T(8,128)(2,1)}) custom-call(bf16[256,640]{1,0:T(8,128)(2,1)} %get-tuple-element.9.refs_0_, bf16[4,64,512]{2,1,0:T(8,128)(2,1)} %get-tuple-element.10.refs_1_, bf16[4,64,512]{2,1,0:T(8,128)(2,1)} %get-tuple-element.11.refs_2_), custom_call_target="tpu_custom_call" | custom-call | bytes 1700000 | tf_op jit(solution)/shard_map/pallas_call | solution.py:738

commit v2 on v1

--- a/solution.py
+++ b/solution.py
@@ -160,6 +160,7 @@
 EXACT = lax.Precision.HIGHEST
 FAR = -1e30
 CHUNKS = 4
+AHEAD = 2
 PLACES = 64
 
 
@@ -181,7 +182,7 @@
     out, k_out, v_out,
     w, w_out, mod8, meta_all, st1, gathered, full, part, relay, parts_in, parts_last,
     st2, st3, qkv, cosine, sine, q_ext, k_ext, v_all, attn, terms, pair_in, summed, moved,
-    arrived, joint, joined, part_v, relay_v, v_in, v_last, lookup, gate,
+    arrived, joint, joined, part_v, relay_v, v_in, v_last, lookup, keys_t, gate,
     w_sem, j_r, pv_s, pv_r, lv_s, lv_r, meta_s, meta_r, st1_s, st1_r, z_s, z_r, f_s, f_r, swap_s, swap_r, p_s, p_r,
     last_s, last_r, st2_s, st2_r, st3_s, st3_r, k_s, k_r, v_s, v_r, a_s, a_r, pair_s, pair_r,
     mv_s, mv_r, ar_s, ar_r,
@@ -246,12 +247,25 @@
     for p in plane:
         copy(meta_all.at[s], meta_all.at[s], meta_s.at[p], meta_r.at[s], p, t).start()
 
-    onehot = (segs[...] == row8).astype(jnp.float32)
+    row32 = lax.broadcasted_iota(jnp.int32, (32, rows), 0)
+    onehot = ((segs[...] == row32 % 8) & (row32 < 24)).astype(jnp.float32).astype(jnp.bfloat16)
     mod8[...] = jnp.zeros(mod8.shape, jnp.float32)
     mod8[:, : modt.shape[1]] = modt[...]
-    shift = dot00(onehot, mod8[0])
-    scale = dot00(onehot, mod8[1])
-    gate[...] = dot00(onehot, mod8[2])
+
+    def modulation(n):
+        whole = mod8[n]
+        high = whole.astype(jnp.bfloat16).astype(jnp.float32)
+        middle = (whole - high).astype(jnp.bfloat16).astype(jnp.float32)
+        low = whole - high - middle
+        parts = jnp.concatenate([high, middle, low, jnp.zeros_like(low)], axis=0)
+        return lax.dot_general(
+            onehot, parts.astype(jnp.bfloat16), (((0,), (0,)), ((), ())),
+            preferred_element_type=jnp.float32,
+        )
+
+    shift = modulation(0)
+    scale = modulation(1)
+    gate[...] = modulation(2)
 
     for p in column:
         copy(st1.at[p], st1.at[p], st1_s.at[p], st1_r.at[p], s, p).wait_recv()
@@ -273,12 +287,14 @@
         theirs = gathered.at[p, chunk(i)]
         return copy(theirs, theirs, z_s.at[i, z], z_r.at[i, p], s, (n_z - 1 - p) * 2 + c)
 
-    for i in range(chunks):
+    def along_z(i):
         for p in line:
             @pl.when(jnp.logical_not(apart(p)))
             def _():
                 own_block(i, p).start()
 
+    for i in range(AHEAD):
+        along_z(i)
     for p in plane:
         copy(meta_all.at[p], meta_all.at[p], meta_s.at[p], meta_r.at[p], p, t).wait_recv()
     lane = lax.broadcasted_iota(jnp.int32, (rows, 128), 1)
@@ -393,15 +409,14 @@
         total = own[i, s].astype(jnp.float32) + got[i, 0].astype(jnp.float32)
         return total + last[i].astype(jnp.float32)
 
-    ones_h = jnp.ones((8, 128), jnp.float32)
+    row_of = lax.broadcasted_iota(jnp.int32, (8, 256), 0)
+    half_of = lax.broadcasted_iota(jnp.int32, (8, 256), 1) // 128
     st2[s] = jnp.zeros((8, rows), jnp.float32)
 
     def collect(i):
         total = summed_head(qk_bufs, i)
         qkv[i] = total
-        q_sq = dot11(ones_h, total[:, :128] * total[:, :128], EXACT)
-        k_sq = dot11(ones_h, total[:, 128:256] * total[:, 128:256], EXACT)
-        st2[s] = jnp.where(row8 == 2 * i, q_sq, jnp.where(row8 == 2 * i + 1, k_sq, st2[s]))
+        st2[s] = st2[s] + dot11((row_of == 2 * i + half_of).astype(jnp.float32), total * total, EXACT)
 
     def collect_v(i, carry):
         v_all[i] = summed_head(v_bufs, i).astype(jnp.bfloat16).reshape(n_seq, cr, 128)
@@ -410,8 +425,8 @@
     load_w.wait()
     load_w_out.wait()
 
-    def during(step, at, work):
-        @pl.when((step >= at) & (step < at + chunks))
+    def during(step, at, work, first=0):
+        @pl.when((step >= at + first) & (step < at + chunks))
         def _():
             work(step - at)
 
@@ -423,6 +438,7 @@
         during(step, 4, collect)
         during(step, 0, tables)
         during(step, 0, from_line)
+        during(step, -AHEAD, along_z, AHEAD)
         return carry
 
     lax.fori_loop(0, chunks + 4, project_step, 0)
@@ -462,28 +478,30 @@
         return copy(mine, k_out.at[:, :, lanes_of(s)], k_s.at[p], k_r.at[s], p, t)
 
     lax.fori_loop(0, chunks, rotate, 0)
-    lax.fori_loop(0, chunks, collect_v, 0)
     for p in column:
         copy(st3.at[p], st3.at[p], st3_s.at[p], st3_r.at[p], s, p).wait_recv()
     norm_rows = lax.rsqrt(jnp.sum(st3[...], axis=0) / all_heads + EPSILON)
 
-    def scale_rows(i, carry):
-        q_col = dot00(norm_rows, (pick == 2 * i).astype(jnp.float32))
-        k_col = dot00(norm_rows, (pick == 2 * i + 1).astype(jnp.float32))
-        q_i = (qkv[i, :, :128] * q_col).astype(jnp.bfloat16)
-        k_i = (qkv[i, :, 128:256] * k_col).astype(jnp.bfloat16)
+    lane_row = lax.broadcasted_iota(jnp.int32, (8, 128), 1)
+    norm_cols = dot00(norm_rows, (pick == lane_row).astype(jnp.float32))
+    for i in range(chunks):
+        q_i = (qkv[i, :, :128] * norm_cols[:, 2 * i : 2 * i + 1]).astype(jnp.bfloat16)
+        k_i = (qkv[i, :, 128:256] * norm_cols[:, 2 * i + 1 : 2 * i + 2]).astype(jnp.bfloat16)
         q_ext[i, :, :, :128] = q_i.reshape(n_seq, cr, 128)
         k_ext[i, :, :, :128] = k_i.reshape(n_seq, cr, 128)
-        return carry
-
-    lax.fori_loop(0, chunks, scale_rows, 0)
+        keys_t[:, i * many : (i + 1) * many] = k_ext[i].reshape(many, 256).T
+    lax.fori_loop(0, chunks, collect_v, 0)
+    for p in plane:
+        send_v(p).start()
+    v_out[:, :, lanes_of(s)] = v_all[:, s]
 
     score_scale = 1.0 / math.sqrt(HEAD_DIM)
 
     def attend(i):
-        keys = k_ext[...].reshape(n_seq * rows, 256)
         values = v_all[...].reshape(n_seq * rows, 128)
-        scores = dot11(q_ext[i].reshape(many, 256), keys)
+        scores = jnp.dot(
+            q_ext[i].reshape(many, 256), keys_t[...], preferred_element_type=jnp.float32
+        )
         top = jnp.max(scores, axis=1, keepdims=True)
         weights = jnp.exp((scores - top) * score_scale)
         denominator = jnp.sum(weights, axis=1, keepdims=True)
@@ -567,16 +585,18 @@
         during(step, 4, join)
         during(step, 3, deliver_all)
         during(step, 2, pair_sum)
+
+        @pl.when(step == chunks + 1)
+        def _():
+            for p in plane:
+                send_k(p).start()
+
         during(step, 0, attend)
         during(step, 1, out_project)
         return carry
 
     lax.fori_loop(0, chunks + 4, attend_step, 0)
-    for p in plane:
-        send_k(p).start()
-        send_v(p).start()
     k_out[:, :, lanes_of(s)] = k_ext[:, s, :, :128]
-    v_out[:, :, lanes_of(s)] = v_all[:, s]
 
     def finish(i, carry):
         for p in line:
@@ -697,6 +717,7 @@
         pltpu.VMEM((chunks, 2, many, 128), bf16),
         pltpu.VMEM((chunks, many, 128), bf16),
         pltpu.VMEM((3 * PLACES, 256), f32),
+        pltpu.VMEM((256, chunks * many), bf16),
         pltpu.VMEM((rows, feats), f32),
         dma((2,)),
         dma((chunks,)),

time: 128 us -> 122 us (0.953)
  the two profiles are of different devices: /device:TPU:14 before, /device:TPU:2 now
where the time goes in v2:
time: 122 us
  Pallas kernels  121 us (99%)
    pallas_call x1, Pallas kernels, fused_body(): pl.pallas_call(functools.partial(fused, n_seq, n_tp, feats * n_tp, heads_...  119 us

profile of v2, /device:TPU:2, one launch (start us, length us, event | category | flops | bytes accessed | tf_op | source)
XLA Modules:
  0.0 121.6 jit_solution(10577081325192709527)
XLA Ops:
  0.6 118.9 %shard_map.112 = (bf16[256,640]{1,0:T(8,128)(2,1)}, bf16[4,64,512]{2,1,0:T(8,128)(2,1)}, bf16[4,64,512]{2,1,0:T(8,128)(2,1)}) custom-call(bf16[256,640]{1,0:T(8,128)(2,1)} %hid.1, s32[1,256]{1,0:T(1,128)} %bitcast.13, s32[3,256]{1,0:T(4,128)} %positions.1, f32[3,4,640]{2,1,0:T(4,128)} %bitcast.10, f32[8,128]{1,0:T(8,128)} %constant.2.clone.freq, ...), custom_call_target="tpu_custom_call" | custom-call | flops 6000000000 | bytes 8000000 | tf_op jit(solution)/shard_map/pallas_call | solution.py:738
  119.5 2.0 %shard_map.113 = (bf16[256,640]{1,0:T(8,128)(2,1)}, bf16[4,64,512]{2,1,0:T(8,128)(2,1)}, bf16[4,64,512]{2,1,0:T(8,128)(2,1)}) custom-call(bf16[256,640]{1,0:T(8,128)(2,1)} %get-tuple-element.9.refs_0_, bf16[4,64,512]{2,1,0:T(8,128)(2,1)} %get-tuple-element.10.refs_1_, bf16[4,64,512]{2,1,0:T(8,128)(2,1)} %get-tuple-element.11.refs_2_), custom_call_target="tpu_custom_call" | custom-call | bytes 1700000 | tf_op jit(solution)/shard_map/pallas_call | solution.py:759

commit v3 on v2

--- a/solution.py
+++ b/solution.py
@@ -450,8 +450,6 @@
         relay_on(v_bufs, i)
         return carry
 
-    lax.fori_loop(0, chunks, relay_v_on, 0)
-
     gains = (q_gain[pl.ds(s, 1), :], k_gain[pl.ds(s, 1), :])
 
     def rotate(i, carry):
@@ -464,6 +462,8 @@
             qkv[i, :, cols] = field * cos_i + swapped * sin_i
         return carry
 
+    lax.fori_loop(0, chunks, rotate, 0)
+    lax.fori_loop(0, chunks - 1, relay_v_on, 0)
     for p in plane:
         copy(st2.at[p], st2.at[p], st2_s.at[p], st2_r.at[p], p, t).wait_recv()
     st3[t] = jnp.sum(st2[...], axis=0)
@@ -477,7 +477,7 @@
         mine = k_ext.at[:, p, :, pl.ds(0, 128)]
         return copy(mine, k_out.at[:, :, lanes_of(s)], k_s.at[p], k_r.at[s], p, t)
 
-    lax.fori_loop(0, chunks, rotate, 0)
+    relay_v_on(chunks - 1, 0)
     for p in column:
         copy(st3.at[p], st3.at[p], st3_s.at[p], st3_r.at[p], s, p).wait_recv()
     norm_rows = lax.rsqrt(jnp.sum(st3[...], axis=0) / all_heads + EPSILON)
@@ -495,7 +495,7 @@
         send_v(p).start()
     v_out[:, :, lanes_of(s)] = v_all[:, s]
 
-    score_scale = 1.0 / math.sqrt(HEAD_DIM)
+    score_scale = math.log2(math.e) / math.sqrt(HEAD_DIM)
 
     def attend(i):
         values = v_all[...].reshape(n_seq * rows, 128)
@@ -503,7 +503,7 @@
             q_ext[i].reshape(many, 256), keys_t[...], preferred_element_type=jnp.float32
         )
         top = jnp.max(scores, axis=1, keepdims=True)
-        weights = jnp.exp((scores - top) * score_scale)
+        weights = jnp.exp2((scores - top) * score_scale)
         denominator = jnp.sum(weights, axis=1, keepdims=True)
         mixed = jnp.dot(weights.astype(jnp.bfloat16), values, preferred_element_type=jnp.float32)
         done = (mixed / denominator).astype(jnp.bfloat16)
@@ -598,23 +598,6 @@
     lax.fori_loop(0, chunks + 4, attend_step, 0)
     k_out[:, :, lanes_of(s)] = k_ext[:, s, :, :128]
 
-    def finish(i, carry):
-        for p in line:
-            theirs = arrived.at[p, i]
-
-            @pl.when(jnp.logical_not(apart(p)))
-            def _():
-                copy(theirs, theirs, ar_s.at[i, p], ar_r.at[i, p], s, p * 2 + c).wait_recv()
-
-        mixed = arrived[0, i].astype(jnp.float32)
-        for p in range(1, n_z):
-            mixed += arrived[p, i].astype(jnp.float32)
-        base = hid[chunk(i), :].astype(jnp.float32)
-        out[chunk(i), :] = (base + gate[chunk(i), :] * mixed).astype(jnp.bfloat16)
-        return carry
-
-    lax.fori_loop(0, chunks, finish, 0)
-
     for p in plane:
         copy(
             k_ext.at[:, p, :, pl.ds(0, 128)], k_out.at[:, :, lanes_of(p)], k_s.at[p], k_r.at[p], p, t
@@ -642,7 +625,6 @@
             def _():
                 block_on(i, p).wait_send()
 
-            to_line(i, p).wait_send()
         for p in plane:
             copy(
                 gathered.at[p, chunk(i)], full.at[c, s, chunk(i)], f_s.at[i, p], f_r.at[i, s], p, t
@@ -653,6 +635,30 @@
         return carry
 
     lax.fori_loop(0, chunks, drain, 0)
+
+    def finish(i, carry):
+        for p in line:
+            theirs = arrived.at[p, i]
+
+            @pl.when(jnp.logical_not(apart(p)))
+            def _():
+                copy(theirs, theirs, ar_s.at[i, p], ar_r.at[i, p], s, p * 2 + c).wait_recv()
+
+        mixed = arrived[0, i].astype(jnp.float32)
+        for p in range(1, n_z):
+            mixed += arrived[p, i].astype(jnp.float32)
+        base = hid[chunk(i), :].astype(jnp.float32)
+        out[chunk(i), :] = (base + gate[chunk(i), :] * mixed).astype(jnp.bfloat16)
+        return carry
+
+    lax.fori_loop(0, chunks, finish, 0)
+
+    def drain_line(i, carry):
+        for p in line:
+            to_line(i, p).wait_send()
+        return carry
+
+    lax.fori_loop(0, chunks, drain_line, 0)
 
 
 def hand_over(*refs):

time: 122 us -> 122 us (level)
  no operation moved by 1% of the time
where the time goes in v3:
time: 122 us; the launch traced here: 121 us
  Pallas kernels  121 us (99%)
    pallas_call x1, Pallas kernels, fused_body(): pl.pallas_call(functools.partial(fused, n_seq, n_tp, feats * n_tp, heads_...  119 us

profile of v3, /device:TPU:2, one launch (start us, length us, event | category | flops | bytes accessed | tf_op | source)
XLA Modules:
  0.0 121.4 jit_solution(12580115854830417384)
XLA Ops:
  0.6 118.7 %shard_map.112 = (bf16[256,640]{1,0:T(8,128)(2,1)}, bf16[4,64,512]{2,1,0:T(8,128)(2,1)}, bf16[4,64,512]{2,1,0:T(8,128)(2,1)}) custom-call(bf16[256,640]{1,0:T(8,128)(2,1)} %hid.1, s32[1,256]{1,0:T(1,128)} %bitcast.13, s32[3,256]{1,0:T(4,128)} %positions.1, f32[3,4,640]{2,1,0:T(4,128)} %bitcast.10, f32[8,128]{1,0:T(8,128)} %constant.2.clone.freq, ...), custom_call_target="tpu_custom_call" | custom-call | flops 6000000000 | bytes 8000000 | tf_op jit(solution)/shard_map/pallas_call | solution.py:744
  119.4 2.0 %shard_map.113 = (bf16[256,640]{1,0:T(8,128)(2,1)}, bf16[4,64,512]{2,1,0:T(8,128)(2,1)}, bf16[4,64,512]{2,1,0:T(8,128)(2,1)}) custom-call(bf16[256,640]{1,0:T(8,128)(2,1)} %get-tuple-element.9.refs_0_, bf16[4,64,512]{2,1,0:T(8,128)(2,1)} %get-tuple-element.10.refs_1_, bf16[4,64,512]{2,1,0:T(8,128)(2,1)} %get-tuple-element.11.refs_2_), custom_call_target="tpu_custom_call" | custom-call | bytes 1700000 | tf_op jit(solution)/shard_map/pallas_call | solution.py:765

commit v4 on v3

--- a/solution.py
+++ b/solution.py
@@ -434,7 +434,11 @@
         during(step, 2, project_qk)
         during(step, 3, functools.partial(relay_on, qk_bufs))
         during(step, 1, from_plane)
-        during(step, 4, project_v)
+        for i in range(chunks):
+            @pl.when(step == chunks + 2 + 2 * i // chunks)
+            def _():
+                project_v(i)
+
         during(step, 4, collect)
         during(step, 0, tables)
         during(step, 0, from_line)
@@ -584,6 +588,7 @@
     def attend_step(step, carry):
         during(step, 4, join)
         during(step, 3, deliver_all)
+        during(step, 0, attend)
         during(step, 2, pair_sum)
 
         @pl.when(step == chunks + 1)
@@ -591,7 +596,6 @@
             for p in plane:
                 send_k(p).start()
 
-        during(step, 0, attend)
         during(step, 1, out_project)
         return carry
 

time: 122 us -> 124 us (1.016)
  the two profiles are of different devices: /device:TPU:2 before, /device:TPU:4 now
where the time goes in v4:
time: 124 us
  Pallas kernels  123 us (99%)
    pallas_call x1, Pallas kernels, fused_body(): pl.pallas_call(functools.partial(fused, n_seq, n_tp, feats * n_tp, heads_...  121 us

profile of v4, /device:TPU:4, one launch (start us, length us, event | category | flops | bytes accessed | tf_op | source)
XLA Modules:
  0.0 123.9 jit_solution(3304626044463551842)
XLA Ops:
  0.6 121.2 %shard_map.112 = (bf16[256,640]{1,0:T(8,128)(2,1)}, bf16[4,64,512]{2,1,0:T(8,128)(2,1)}, bf16[4,64,512]{2,1,0:T(8,128)(2,1)}) custom-call(bf16[256,640]{1,0:T(8,128)(2,1)} %hid.1, s32[1,256]{1,0:T(1,128)} %bitcast.13, s32[3,256]{1,0:T(4,128)} %positions.1, f32[3,4,640]{2,1,0:T(4,128)} %bitcast.10, f32[8,128]{1,0:T(8,128)} %constant.2.clone.freq, ...), custom_call_target="tpu_custom_call" | custom-call | flops 6000000000 | bytes 8000000 | tf_op jit(solution)/shard_map/pallas_call | solution.py:748
  121.8 2.0 %shard_map.113 = (bf16[256,640]{1,0:T(8,128)(2,1)}, bf16[4,64,512]{2,1,0:T(8,128)(2,1)}, bf16[4,64,512]{2,1,0:T(8,128)(2,1)}) custom-call(bf16[256,640]{1,0:T(8,128)(2,1)} %get-tuple-element.9.refs_0_, bf16[4,64,512]{2,1,0:T(8,128)(2,1)} %get-tuple-element.10.refs_1_, bf16[4,64,512]{2,1,0:T(8,128)(2,1)} %get-tuple-element.11.refs_2_), custom_call_target="tpu_custom_call" | custom-call | bytes 1700000 | tf_op jit(solution)/shard_map/pallas_call | solution.py:769
